TPU v7x, 256 devices: a whole 4x4x8 slice. The times are simulated.
256 devices in a mesh: shot: 64 (over x, y, z_lo, core), head: 4 (over z_hi).
Axes of the slice: x: 4, y: 4, z: 8 (z_hi: 4, z_lo: 2; z = z_hi * 2 + z_lo), core: 2. Of those that a mesh axis runs over, the one named last changes fastest.
Arguments:
- summary_states: bfloat16 [1024, 4096], P('shot', 'head'), may hold values from -6 to 6
- summary_queries: bfloat16 [1024, 4096], P('shot', 'head'), may hold values from -360 to 360
- summary_keys: bfloat16 [1024, 4096], P('shot', 'head'), may hold values from -6 to 6
- summary_values: bfloat16 [1024, 4096], P('shot', 'head'), may hold values from -6 to 6
- demo_keys: bfloat16 [128, 512, 4096], P('shot', None, 'head'), may hold values from -6 to 6
- demo_values: bfloat16 [128, 512, 4096], P('shot', None, 'head'), may hold values from -6 to 6
- demo_lengths: int32 [128], P('shot'), may hold values from 128 to 512
- out_weight: bfloat16 [4096, 4096], P('head', 'shot'), may hold values from -0.09375 to 0.09375
- norm_gain: float32 [4096], P('head'), may hold values from 0.5 to 1.5
- key_weight: bfloat16 [4096, 4096], P('shot', 'head'), may hold values from -0.09375 to 0.09375
- value_weight: bfloat16 [4096, 4096], P('shot', 'head'), may hold values from -0.09375 to 0.09375
- query_queries: bfloat16 [65536, 4096], P('shot', 'head'), may hold values from -360 to 360
- query_keys: bfloat16 [65536, 4096], P('shot', 'head'), may hold values from -6 to 6
- query_values: bfloat16 [65536, 4096], P('shot', 'head'), may hold values from -6 to 6
- query_offsets: int32 [512], P('shot'), may hold values from 0 to 128
Outputs:
- answer: bfloat16 [65536, 4096], P('shot', 'head')
All inputs are finite; a program needn't handle non-finite values.
Results may differ from a plain program's by a relative error of at most 0.024.
Values may be sent and summed in bfloat16 or wider, within the bound.
No kernel may reach another device: no remote copies, remote signals or barrier semaphores. Data moves between devices by JAX's collectives and lax.ppermute only.
A program may use at most 128 MiB of HBM per device.

v0:
```python
import jax
import jax.numpy as jnp
from jax import lax
from jax.sharding import PartitionSpec as P

D = 4096
HD = 128
SLOTS = 8
QLEN = 128


NEG = -1e30
EPS = 1e-05


def per_device(
    summary_states,
    summary_queries,
    summary_keys,
    summary_values,
    demo_keys,
    demo_values,
    demo_lengths,
    out_weight,
    norm_gain,
    key_weight,
    value_weight,
    query_queries,
    query_keys,
    query_values,
    query_offsets,
):
    scale = HD ** (-0.5)
    f32 = jnp.float32
    rows_local = summary_states.shape[0]
    width_local = summary_states.shape[1]
    local_heads = width_local // HD
    demo_local = demo_keys.shape[0]
    cache_len = demo_keys.shape[1]
    qs = summary_queries.reshape(demo_local, SLOTS, local_heads, HD)
    ks = summary_keys.reshape(demo_local, SLOTS, local_heads, HD)
    vs = summary_values.reshape(demo_local, SLOTS, local_heads, HD)
    kc = demo_keys.reshape(demo_local, cache_len, local_heads, HD)
    vc = demo_values.reshape(demo_local, cache_len, local_heads, HD)
    cache_scores = jnp.einsum("dshe,dlhe->dhsl", qs, kc, preferred_element_type=f32) * scale
    own_scores = jnp.einsum("dshe,dthe->dhst", qs, ks, preferred_element_type=f32) * scale
    cache_mask = (jnp.arange(cache_len)[None, :] < demo_lengths[:, None])[:, None, None, :]
    own_mask = jnp.tril(jnp.ones((SLOTS, SLOTS), bool))[None, None]
    top = jnp.maximum(
        jnp.max(jnp.where(cache_mask, cache_scores, NEG), -1),
        jnp.max(jnp.where(own_mask, own_scores, NEG), -1),
    )
    w_cache = jnp.where(cache_mask, jnp.exp(cache_scores - top[..., None]), 0.0)
    w_own = jnp.where(own_mask, jnp.exp(own_scores - top[..., None]), 0.0)
    numer = jnp.einsum(
        "dhsl,dlhe->dshe", w_cache.astype(jnp.bfloat16), vc, preferred_element_type=f32
    )
    numer = numer + jnp.einsum(
        "dhst,dthe->dshe", w_own.astype(jnp.bfloat16), vs, preferred_element_type=f32
    )
    denom = (jnp.sum(w_cache, -1) + jnp.sum(w_own, -1)).transpose(0, 2, 1)[..., None]
    compressed = (numer / denom).astype(jnp.bfloat16).reshape(rows_local, width_local)
    partial_out = jnp.dot(
        compressed,
        lax.all_gather(out_weight, "shot", axis=1, tiled=True),
        preferred_element_type=f32,
    )
    attended = lax.psum_scatter(partial_out, "head", scatter_dimension=1, tiled=True)
    mixed = summary_states.astype(f32) + attended
    power = lax.psum(jnp.sum(mixed * mixed, axis=1), "head")
    normed = (mixed * lax.rsqrt(power / D + EPS)[:, None] * norm_gain[None, :]).astype(jnp.bfloat16)
    full_rows = lax.all_gather(normed, "head", axis=1, tiled=True)
    key_sum = jnp.dot(
        full_rows,
        lax.all_gather(key_weight, "shot", axis=0, tiled=True),
        preferred_element_type=f32,
    )
    value_sum = jnp.dot(
        full_rows,
        lax.all_gather(value_weight, "shot", axis=0, tiled=True),
        preferred_element_type=f32,
    )
    compact_keys = key_sum.astype(jnp.bfloat16)
    compact_values = value_sum.astype(jnp.bfloat16)
    query_rows = query_queries.shape[0]
    examples = query_rows // QLEN
    reach = jnp.repeat(query_offsets, QLEN)
    q_heads = query_queries.reshape(query_rows, local_heads, HD).transpose(1, 0, 2)
    k_heads = query_keys.reshape(query_rows, local_heads, HD).transpose(1, 0, 2)
    v_heads = query_values.reshape(query_rows, local_heads, HD).transpose(1, 0, 2)
    q_ex = q_heads.reshape(local_heads, examples, QLEN, HD)
    k_ex = k_heads.reshape(local_heads, examples, QLEN, HD)
    v_ex = v_heads.reshape(local_heads, examples, QLEN, HD)
    near = jnp.einsum("hexd,heyd->hexy", q_ex, k_ex, preferred_element_type=f32) * scale
    causal = jnp.tril(jnp.ones((QLEN, QLEN), bool))[None, None]
    start_top = jnp.max(jnp.where(causal, near, NEG), -1)
    w_near = jnp.where(causal, jnp.exp(near - start_top[..., None]), 0.0)
    start_sum = jnp.sum(w_near, -1).reshape(local_heads, query_rows)
    start_acc = jnp.einsum(
        "hexy,heyd->hexd", w_near.astype(jnp.bfloat16), v_ex, preferred_element_type=f32
    ).reshape(local_heads, query_rows, HD)
    start_top = start_top.reshape(local_heads, query_rows)
    keys_piece = lax.all_gather(compact_keys, "shot", axis=0, tiled=True)
    values_piece = lax.all_gather(compact_values, "shot", axis=0, tiled=True)
    count = keys_piece.shape[0]
    kp = keys_piece.reshape(count, local_heads, HD).transpose(1, 0, 2)
    vp = values_piece.reshape(count, local_heads, HD).transpose(1, 0, 2)
    allowed = (jnp.arange(count) // SLOTS)[None, :] < reach[:, None]

    def one_head(items):
        qh, kh, vh, best, total, acc = items
        far = jnp.einsum("qe,pe->qp", qh, kh, preferred_element_type=f32) * scale
        new_best = jnp.maximum(best, jnp.max(jnp.where(allowed, far, NEG), -1))
        weights = jnp.where(allowed, jnp.exp(far - new_best[:, None]), 0.0)
        factor = jnp.exp(best - new_best)
        new_total = total * factor + jnp.sum(weights, -1)
        new_acc = acc * factor[:, None] + jnp.dot(
            weights.astype(jnp.bfloat16), vh, preferred_element_type=f32
        )
        return (new_best, new_total, new_acc)

    final_top, final_sum, final_acc = lax.map(
        one_head, (q_heads, kp, vp, start_top, start_sum, start_acc)
    )
    answer = (final_acc / final_sum[..., None]).astype(jnp.bfloat16)
    return answer.transpose(1, 0, 2).reshape(query_rows, width_local)


def solution(mesh):
    return jax.shard_map(
        per_device,
        mesh=mesh,
        in_specs=(
            P("shot", "head"),
            P("shot", "head"),
            P("shot", "head"),
            P("shot", "head"),
            P("shot", None, "head"),
            P("shot", None, "head"),
            P("shot"),
            P("head", "shot"),
            P("head"),
            P("shot", "head"),
            P("shot", "head"),
            P("shot", "head"),
            P("shot", "head"),
            P("shot", "head"),
            P("shot"),
        ),
        out_specs=P("shot", "head"),
        check_vma=False,
    )
```

profile of v0, /device:TPU:1, one launch (start us, length us, event | category | flops | bytes accessed | tf_op | source)
XLA Modules:
  0.0 687.8 jit_solution(5534283498446392165)
XLA Ops:
  9.0 1.5 select_reduce_fusion.1
  10.7 2.1 fusion.35
  12.8 114.2 %all-gather.6.cloned.1.call-done = bf16[1024,4096]{0,1:T(8,128)(2,1)} async-done(((bf16[1024,64]{0,1:T(8,128)(2,1)}), bf16[1024,4096]{0,1:T(8,128)(2,1)}) %all-gather.6.cloned.1.call-update) | async-done | bytes 8388624 | tf_op jit(solution)/shard_map/all_gather | solution.py:65
  127.1 6.5 fusion.53
  135.0 21.0 %reduce-scatter.2.cloned.1.call-done = f32[16,1024]{1,0:T(8,128)} async-done(((f32[16,4096]{1,0:T(8,128)}), f32[16,1024]{1,0:T(8,128)}) %reduce-scatter.2.cloned.1.call-update) | async-done | bytes 65552 | tf_op jit(solution)/shard_map/reduce_scatter | solution.py:68
  156.9 10.1 %psum.7 = f32[16]{0:T(128)S(1)} all-reduce(f32[16]{0:T(128)S(1)} %multiply_reduce_fusion), channel_id=1, replica_groups=mesh['shot'=64,'head'=4] {'head'}, use_global_device_ids=true, to_apply=%region_6.7 | all-reduce | flops 16 | bytes 128 | tf_op jit(solution)/shard_map/psum | solution.py:70
  167.9 11.2 %all_gather.19 = bf16[16,4096]{1,0:T(8,128)(2,1)S(1)} all-gather(bf16[16,1024]{1,0:T(8,128)(2,1)S(1)} %multiply_convert_fusion), channel_id=1, replica_groups=mesh['shot'=64,'head'=4] {'head'}, dimensions={1}, use_global_device_ids=true | all-gather | bytes 163840 | tf_op jit(solution)/shard_map/all_gather | solution.py:72
  179.1 93.7 %all-gather.8.cloned.1.call-done = bf16[4096,1024]{1,0:T(8,128)(2,1)} async-done(((bf16[64,1024]{1,0:T(8,128)(2,1)}), bf16[4096,1024]{1,0:T(8,128)(2,1)}) %all-gather.8.cloned.1.call-update) | async-done | bytes 8388624 | tf_op jit(solution)/shard_map/all_gather | solution.py:75
  272.8 5.2 convolution_convert_fusion.1
  278.2 109.0 %all-gather.12.cloned.1.call-done = bf16[4096,1024]{1,0:T(8,128)(2,1)} async-done(((bf16[64,1024]{1,0:T(8,128)(2,1)}), bf16[4096,1024]{1,0:T(8,128)(2,1)}) %all-gather.12.cloned.1.call-update) | async-done | bytes 8388624 | tf_op jit(solution)/shard_map/all_gather | solution.py:80
  387.2 5.2 convolution_convert_fusion
  392.4 2.9 copy.37
  395.3 2.4 copy.51
  397.6 2.4 copy.57
  401.9 1.6 select_reduce_fusion
  403.6 1.1 fusion.32
  404.7 3.0 fusion.33
  407.8 86.2 %all-gather.10.cloned.1.call-done = bf16[1024,1024]{1,0:T(8,128)(2,1)} async-done(((bf16[16,1024]{1,0:T(8,128)(2,1)}), bf16[1024,1024]{1,0:T(8,128)(2,1)}) %all-gather.10.cloned.1.call-update) | async-done | bytes 2097168 | tf_op jit(solution)/shard_map/all_gather | solution.py:103
  494.0 2.0 bitcast_bitcast_fusion.1
  495.9 104.4 %all-gather.14.cloned.1.call-done = bf16[1024,1024]{1,0:T(8,128)(2,1)} async-done(((bf16[16,1024]{1,0:T(8,128)(2,1)}), bf16[1024,1024]{1,0:T(8,128)(2,1)}) %all-gather.14.cloned.1.call-update) | async-done | bytes 2097168 | tf_op jit(solution)/shard_map/all_gather | solution.py:104
  600.3 3.3 bitcast_bitcast_fusion
  603.6 73.4 %while.13 = (s32[]{:T(128)}, f32[8,1024]{1,0:T(8,128)S(1)}, f32[8,1024,128]{2,1,0:T(8,128)}, f32[8,1024]{1,0:T(8,128)S(1)}, f32[8,1024]{1,0:T(8,128)S(1)}, /*ind...) while((s32[]{:T(128)}, f32[8,1024]{1,0:T(8,128)S(1)}, ...), condition=%wide.region_12.13_spmd.clone, body=%wide.region_9.12_spmd.clone.sunk | while | flops 551817216 | bytes 31295660 | solution.py:122
  603.6 1.7 fusion.105
  605.4 1.9 copy-done.2
  607.3 1.0 fusion.106
  608.4 4.4 fusion.108
  612.8 1.7 fusion.105
  614.5 1.9 copy-done.2
  617.6 4.4 fusion.108
  622.0 1.7 fusion.105
  623.7 1.9 copy-done.2
  626.8 4.4 fusion.108
  631.2 1.7 fusion.105
  632.9 1.9 copy-done.2
  635.9 4.4 fusion.108
  640.3 1.7 fusion.105
  642.1 1.9 copy-done.2
  645.1 4.4 fusion.108
  649.5 1.7 fusion.105
  651.2 1.9 copy-done.2
  654.3 4.4 fusion.108
  658.7 1.7 fusion.105
  660.4 1.9 copy-done.2
  663.4 4.4 fusion.108
  667.8 1.7 fusion.105
  669.5 1.9 copy-done.2
  672.6 4.4 fusion.108
  677.0 4.0 copy_bitcast_fusion
  (94 shorter events, 16.1 us)
Async XLA Ops:
  6.5 2.5 copy-start
  6.5 120.5 %copy-start.6 = (bf16[16,1024]{1,0:T(8,128)(2,1)S(1)}, bf16[16,1024]{1,0:T(8,128)(2,1)}, u32[]{:S(2)}) copy-start(bf16[16,1024]{1,0:T(8,128)(2,1)} %param.20) | copy-start | bytes 98308
  6.5 120.5 %all-gather.6.cloned.1.call-start = ((), (), s32[]{:S(2)}) async-start(), calls=%async_computation.1 | async-start | bytes 8519680 | tf_op jit(solution)/shard_map/all_gather | solution.py:65
  7.3 148.7 %reduce-scatter.2.cloned.1.call-start = ((), (), s32[]{:S(2)}) async-start(), calls=%async_computation.2 | async-start | bytes 327680 | tf_op jit(solution)/shard_map/reduce_scatter | solution.py:68
  12.8 143.1 %copy-start.5 = (bf16[16,1024]{1,0:T(8,128)(2,1)S(1)}, bf16[16,1024]{1,0:T(8,128)(2,1)}, u32[]{:S(2)}) copy-start(bf16[16,1024]{1,0:T(8,128)(2,1)} %param.17) | copy-start | bytes 98308
  12.8 154.2 %copy-start.7 = (f32[1024]{0:T(1024)S(1)}, f32[1024]{0:T(1024)}, u32[]{:S(2)}) copy-start(f32[1024]{0:T(1024)} %param.25) | copy-start | bytes 12292
  133.6 139.2 %all-gather.8.cloned.1.call-start = ((), (), s32[]{:S(2)}) async-start(), calls=%async_computation.3 | async-start | bytes 8519680 | tf_op jit(solution)/shard_map/all_gather | solution.py:75
  134.3 252.8 %all-gather.12.cloned.1.call-start = ((), (), s32[]{:S(2)}) async-start(), calls=%async_computation.5 | async-start | bytes 8519680 | tf_op jit(solution)/shard_map/all_gather | solution.py:80
  134.9 359.0 %all-gather.10.cloned.1.call-start = ((), (), s32[]{:S(2)}) async-start(), calls=%async_computation.4 | async-start | bytes 2129920 | tf_op jit(solution)/shard_map/all_gather | solution.py:103
  278.0 322.3 %all-gather.14.cloned.1.call-start = ((), (), s32[]{:S(2)}) async-start(), calls=%async_computation.6 | async-start | bytes 2129920 | tf_op jit(solution)/shard_map/all_gather | solution.py:104
  397.6 2.7 copy-start.4
  400.3 1.0 copy-start.8
  400.3 1.6 copy-start.3
  605.3 2.0 copy-start.2
  614.5 2.0 copy-start.2
  623.7 2.0 copy-start.2
  632.9 2.0 copy-start.2
  642.0 2.0 copy-start.2
  651.2 2.0 copy-start.2
  660.4 2.0 copy-start.2
  669.5 2.0 copy-start.2
  677.0 4.0 copy-start.1
Sparse Core Ops, SparseCore 0:
  9.2 117.7 all-gather.5
  133.7 22.1 reduce-scatter.1
  157.9 114.7 all-gather.7
  274.7 112.4 all-gather.11
  389.0 104.8 all-gather.9
  495.8 104.4 all-gather.13
where the time goes:
time: 689 us; the launch traced here: 688 us
  waiting for transfers between devices  530 us (77%)
  matrix products  74.6 us (11%)
  local copies, waits for them, and re-layouts  31 us (4%)
  blocking collectives  21.3 us (3%)
  other arithmetic  16.1 us (2%)
  between operations  13.7 us (2%)
    all_gather x1, waiting for transfers between devices, per_device(): lax.all_gather(out_weight, 'shot', axis=1, tiled=True)  114 us
    all_gather x1, waiting for transfers between devices, per_device(): lax.all_gather(value_weight, 'shot', axis=0, tiled=True)  109 us
    all_gather x1, waiting for transfers between devices, per_device(): values_piece = lax.all_gather(compact_values, 'shot', axis=0, tiled=True)  104 us
    all_gather x1, waiting for transfers between devices, per_device(): lax.all_gather(key_weight, 'shot', axis=0, tiled=True)  93.7 us
    all_gather x1, waiting for transfers between devices, per_device(): keys_piece = lax.all_gather(compact_keys, 'shot', axis=0, tiled=True)  86.2 us
    dot_general x8, matrix products, one_head(): jnp.dot(weights.astype(jnp.bfloat16), vh, preferred_element_type=f32)  35.1 us
    reduce_scatter x1, waiting for transfers between devices, per_device(): lax.psum_scatter(partial_out, 'head', scatter_dimension=1, tiled=True)  21 us
    while x16, local copies, waits for them, and re-layouts  15.3 us
  transfers between devices with their start and end apart: 6, of which 6 were waited for; matrix products, arithmetic and copies ran while one was open for 5% of the time, Pallas kernels for 0%

commit v1 on v0

v1 whole, which is shorter than its diff:
```python
import functools
import math

import jax
import jax.numpy as jnp
from jax import lax
from jax.experimental import pallas as pl
from jax.experimental.pallas import tpu as pltpu
from jax.sharding import PartitionSpec as P

D = 4096
HD = 128
SLOTS = 8
QLEN = 128
HEADS = 8
WIDTH = HEADS * HD
HALF = WIDTH // 2
NEG = -1e30
EPS = 1e-05
EXPO = HD ** (-0.5) * math.log2(math.e)

f32 = jnp.float32
bf16 = jnp.bfloat16
VM = pl.BlockSpec(memory_space=pltpu.VMEM)
SM = pl.BlockSpec(memory_space=pltpu.SMEM)
ANY = pl.BlockSpec(memory_space=pl.ANY)
NT = (((1,), (1,)), ((), ()))
TN = (((0,), (0,)), ((), ()))
NN = (((1,), (0,)), ((), ()))


SMALL = pl.CostEstimate(flops=1000, bytes_accessed=1000, transcendentals=0)
LARGE = pl.CostEstimate(flops=int(5e10), bytes_accessed=1000, transcendentals=0)


def dot(a, b, dims=NN):
    return lax.dot_general(a, b, dims, preferred_element_type=f32)


def shape(dims, dtype=bf16):
    return jax.ShapeDtypeStruct(dims, dtype)


def call(kernel, outs, n_in, scratch=(), mb=24):
    return pl.pallas_call(
        kernel,
        out_shape=outs,
        in_specs=[SM] + [VM] * n_in,
        out_specs=jax.tree.map(lambda _: VM, outs),
        scratch_shapes=list(scratch),
        cost_estimate=SMALL,
        compiler_params=pltpu.CompilerParams(vmem_limit_bytes=mb << 20),
    )


def after(v, *others):
    return lax.optimization_barrier((v, *others))[0]


def places():
    return [(i >> 4, (i >> 2) & 3, (i >> 1) & 1, i & 1) for i in range(64)]


def index(x, y, z, c):
    return (((x & 3) * 4 + (y & 3)) * 2 + z) * 2 + c


def send(v, to):
    return lax.ppermute(v, "shot", [(i, index(*to(*p))) for i, p in enumerate(places())])


def send_x(v, k):
    return send(v, lambda x, y, z, c: (x + k, y, z, c))


def send_y(v, k):
    return send(v, lambda x, y, z, c: (x, y + k, z, c))


def send_z(v):
    return send(v, lambda x, y, z, c: (x, y, 1 - z, c))


def send_core(v):
    return send(v, lambda x, y, z, c: (x, y, z, 1 - c))


def turn(c, back):
    return (1 - 2 * c) * (-1 if back else 1)


def ring(v, move):
    first = send(v, lambda x, y, z, c: move(x, y, z, c, turn(c, False)))
    second = send(v, lambda x, y, z, c: move(x, y, z, c, turn(c, True)))
    return first, second, lambda u: send(u, lambda x, y, z, c: move(x, y, z, c, turn(c, False)))


def ring_y(v):
    return ring(v, lambda x, y, z, c, k: (x, y + k, z, c))


def ring_head(v):
    def step(u, back):
        pairs = [(i * 4 + h, i * 4 + (h + turn(i & 1, back)) % 4) for i in range(64) for h in range(4)]
        return lax.ppermute(u, ("shot", "head"), pairs)

    first = step(v, False)
    return [first, step(v, True), step(first, False)]


def write_aside(at_ref, states_ref, gain_ref, keep_ref, give_ref, rows_ref):
    y, z, core = at_ref[1], at_ref[2], at_ref[3]
    low = lax.broadcasted_iota(jnp.int32, (16, HD), 1) < HD // 2
    row = lax.broadcasted_iota(jnp.int32, (16, HD), 0)

    def pick(ref, at_z):
        def block(step):
            start = ((y + step) & 3) * 256 + at_z * HD
            return jnp.broadcast_to(ref[:, pl.ds(pl.multiple_of(start, HD), HD)].astype(f32), (16, HD))

        here, back, ahead, over = block(0), block(-1), block(1), block(2)

        def lows(a, b):
            return jnp.where(low, a, pltpu.roll(b, HD // 2, 1))

        def highs(a, b):
            return jnp.where(low, pltpu.roll(a, HD // 2, 1), b)

        zero = [lows(here, back), lows(ahead, over)]
        one = [highs(here, ahead), highs(back, over)]
        return [jnp.where(core == 0, a, b) for a, b in zip(zero + one, one + zero)]

    for k, v in enumerate(pick(states_ref, z)):
        keep_ref[:, WIDTH + k * HD : WIDTH + (k + 1) * HD] = v.astype(bf16)
    for k, v in enumerate(pick(states_ref, 1 - z)):
        give_ref[:, WIDTH + k * HD : WIDTH + (k + 1) * HD] = v.astype(bf16)
    for k, gain in enumerate(pick(gain_ref, z)):
        high = gain.astype(bf16).astype(f32)
        both = jnp.where(row == 0, high, jnp.where(row == 1, gain - high, 0.0))
        rows_ref[:, k * HD : (k + 1) * HD] = both.astype(bf16)


def demo_kernel(
    len_ref, at_ref, q_ref, ks_ref, vs_ref, kc_ref, vc_ref, states_ref, gain_ref, keep_ref, give_ref, rows_ref, total
):
    d = pl.program_id(0)

    @pl.when(d == 0)
    def _():
        write_aside(at_ref, states_ref, gain_ref, keep_ref, give_ref, rows_ref)

    q = q_ref[...].astype(f32)
    mine = jnp.where(d == 0, q[:SLOTS], q[SLOTS:])
    rows = lax.broadcasted_iota(jnp.int32, (HEADS * SLOTS, WIDTH), 0) // SLOTS
    cols = lax.broadcasted_iota(jnp.int32, (HEADS * SLOTS, WIDTH), 1) // HD
    same = rows == cols
    qe = jnp.where(same, jnp.concatenate([mine] * HEADS, axis=0), 0.0).astype(bf16)
    kc = kc_ref[0]
    s = dot(kc, qe, NT)
    so = dot(ks_ref[...], qe, NT)
    at = lax.broadcasted_iota(jnp.int32, s.shape, 0)
    s = jnp.where(at < len_ref[d], s, NEG)
    t = lax.broadcasted_iota(jnp.int32, so.shape, 0)
    slot = lax.broadcasted_iota(jnp.int32, so.shape, 1) % SLOTS
    so = jnp.where((t // SLOTS == d) & (t % SLOTS <= slot), so, NEG)
    top = jnp.maximum(jnp.max(s, 0, keepdims=True), jnp.max(so, 0, keepdims=True))
    p = jnp.exp2((s - top) * EXPO).astype(bf16)
    po = jnp.exp2((so - top) * EXPO).astype(bf16)
    num = dot(p, vc_ref[0], TN) + dot(po, vs_ref[...], TN)
    den = dot(p, jnp.ones((p.shape[0], HD), bf16), TN) + dot(po, jnp.ones((po.shape[0], HD), bf16), TN)
    res = jnp.where(same, num / jnp.concatenate([den] * HEADS, axis=1), 0.0)
    total[pl.ds(pl.multiple_of(d * SLOTS, SLOTS), SLOTS), :] = jnp.sum(res.reshape(HEADS, SLOTS, WIDTH), axis=0)

    @pl.when(d == pl.num_programs(0) - 1)
    def _():
        keep_ref[:, :WIDTH] = total[...].astype(bf16)
        give_ref[:, :WIDTH] = total[...].astype(bf16)


def demo_attention(lengths, at, q, ks, vs, kc, vc, states, gain):
    n, length, _ = kc.shape
    rows = q.shape[0]
    whole = pl.BlockSpec((rows, WIDTH), lambda i, *_: (0, 0))
    cached = pl.BlockSpec((1, length, WIDTH), lambda i, *_: (i, 0, 0))
    return pl.pallas_call(
        demo_kernel,
        out_shape=(shape((rows, WIDTH + HALF)), shape((rows, WIDTH + HALF)), shape((rows, HALF))),
        grid_spec=pltpu.PrefetchScalarGridSpec(
            num_scalar_prefetch=2,
            grid=(n,),
            in_specs=[whole, whole, whole, cached, cached, whole, pl.BlockSpec((1, WIDTH), lambda i, *_: (0, 0))],
            out_specs=[
                pl.BlockSpec((rows, WIDTH + HALF), lambda i, *_: (0, 0)),
                pl.BlockSpec((rows, WIDTH + HALF), lambda i, *_: (0, 0)),
                pl.BlockSpec((rows, HALF), lambda i, *_: (0, 0)),
            ],
            scratch_shapes=[pltpu.VMEM((rows, WIDTH), f32)],
        ),
        cost_estimate=SMALL,
        compiler_params=pltpu.CompilerParams(vmem_limit_bytes=60 << 20),
    )(lengths, at, q, ks, vs, kc, vc, states, gain.reshape(1, WIDTH))


def eye(n):
    row = lax.broadcasted_iota(jnp.int32, (n, n), 0)
    col = lax.broadcasted_iota(jnp.int32, (n, n), 1)
    return (row == col).astype(f32).astype(bf16)


def near_kernel(group, at_ref, q_ref, k_ref, v_ref, *refs):
    row = lax.broadcasted_iota(jnp.int32, (QLEN, QLEN), 0)
    col = lax.broadcasted_iota(jnp.int32, (QLEN, QLEN), 1)
    causal = row <= col
    o_ref, l_ref = refs[-2:]
    cuts = [slice(j * HD, (j + 1) * HD) for j in range(HEADS)]
    for e in range(group):
        to = slice(e * QLEN, (e + 1) * QLEN)
        scores = [jnp.where(causal, dot(k_ref[to, at], q_ref[to, at], NT), NEG) for at in cuts]
        tops = [jnp.max(s, 0, keepdims=True) * EXPO for s in scores]
        weights = [jnp.exp2(s * EXPO - top) for s, top in zip(scores, tops)]
        dens = [jnp.sum(p, 0, keepdims=True) for p in weights]
        sums = [dot(v_ref[to, at], p.astype(bf16), TN) for p, at in zip(weights, cuts)]
        for j, at in enumerate(cuts):
            o_ref[0, at, to] = (sums[j] * (1.0 / dens[j])).astype(bf16)
            l_ref[0, j : j + 1, to] = tops[j] + jnp.log2(dens[j])


def state_shapes(q, group):
    return shape((q.shape[0] // (group * QLEN), WIDTH, group * QLEN)), shape(
        (q.shape[0] // (group * QLEN), HEADS, group * QLEN), f32
    )


def state_specs(group):
    return [
        pl.BlockSpec((1, WIDTH, group * QLEN), lambda g: (g, 0, 0)),
        pl.BlockSpec((1, HEADS, group * QLEN), lambda g: (g, 0, 0)),
    ]


def query_spec(group):
    return pl.BlockSpec((group * QLEN, WIDTH), lambda g: (g, 0))


def near_attention(at, q, k, v, begin, count, state=(), group=2):
    block = pl.BlockSpec((group * QLEN, WIDTH), lambda g: (g + begin, 0))
    return pl.pallas_call(
        functools.partial(near_kernel, group),
        out_shape=state_shapes(q, group),
        grid=(count,),
        in_specs=[SM] + [block] * 3 + [ANY] * len(state),
        out_specs=[
            pl.BlockSpec((1, WIDTH, group * QLEN), lambda g: (g + begin, 0, 0)),
            pl.BlockSpec((1, HEADS, group * QLEN), lambda g: (g + begin, 0, 0)),
        ],
        input_output_aliases={4 + i: i for i in range(len(state))},
        cost_estimate=LARGE,
        compiler_params=pltpu.CompilerParams(vmem_limit_bytes=58 << 20),
    )(at, q, k, v, *state)


def out_kernel(at_ref, *refs):
    c, w, (g_ref, own_ref, give_ref) = refs[:4], refs[4:12], refs[12:]
    mine = (at_ref[4] == at_ref[0]).astype(f32)
    rows = jnp.concatenate([r[:, :WIDTH] for r in c], axis=0)
    cols = jnp.concatenate([r[...] for r in w], axis=0)
    states = jnp.concatenate([r[:, WIDTH:] for r in c], axis=0).astype(f32)
    total = dot(rows, cols, NT) + states * mine
    gain = g_ref[...].astype(f32) * mine
    own_ref[:128, :] = total
    own_ref[128:, :] = gain
    give_ref[:128, :] = total.astype(bf16)
    give_ref[128:, :] = gain.astype(bf16)


def spread(power):
    lane = lax.broadcasted_iota(jnp.int32, (power.shape[0], HD), 1)
    high = power.astype(bf16).astype(f32)
    return jnp.where(lane == 0, high, jnp.where(lane == 1, power - high, 0.0)).astype(bf16)


WIDE = 2 * WIDTH + HD


def project_kernel(at_ref, own_ref, a_ref, b_ref, c_ref, *refs):
    w, outs = refs[:8], refs[8:]
    total = own_ref[...] + a_ref[...].astype(f32) + b_ref[...].astype(f32) + c_ref[...].astype(f32)
    gain = total[128:129, :] + total[129:130, :]
    mixed = total[:128, :]
    power = jnp.sum(mixed * mixed, axis=1, keepdims=True)
    y = (mixed * gain).astype(bf16)
    lane = lax.broadcasted_iota(jnp.int32, (32, HD), 1)
    for side in range(2):
        to = slice(side * WIDTH, (side + 1) * WIDTH)
        res = dot(y, jnp.concatenate([r[64 * side : 64 * side + 64, :] for r in w], axis=0))
        for k, r in enumerate(outs):
            r[:, to] = res[k * 32 : (k + 1) * 32, :].astype(r.dtype)
    for k, r in enumerate(outs):
        part = power[k * 32 : (k + 1) * 32, :]
        r[:, 2 * WIDTH :] = jnp.where(lane == 0, part, 0.0) if k == 0 else spread(part)


def half_kernel(at_ref, own_ref, a_ref, b_ref, c_ref, keep_ref, give_ref):
    total = own_ref[...] + a_ref[...].astype(f32) + b_ref[...].astype(f32) + c_ref[...].astype(f32)
    keep_ref[...] = total
    give_ref[:, : 2 * WIDTH] = total[:, : 2 * WIDTH].astype(bf16)
    give_ref[:, 2 * WIDTH :] = spread(jnp.sum(total[:, 2 * WIDTH :], axis=1, keepdims=True))


def compact_kernel(at_ref, own_ref, a_ref, keep_ref, give_ref):
    core = at_ref[3]
    total = own_ref[...] + a_ref[...].astype(f32)
    power = jnp.sum(total[:, 2 * WIDTH :], axis=1, keepdims=True)
    factor = lax.rsqrt(power / D + EPS)
    keys, values = total[:, :WIDTH] * factor, total[:, WIDTH : 2 * WIDTH] * factor
    keep_ref[...] = jnp.where(core == 0, keys, values).astype(bf16)
    give_ref[...] = jnp.where(core == 0, values, keys).astype(bf16)


STEP = (0, -1, 1, 2)


def far_kernel(chunks, last, group, ahead, at_ref, off_ref, q_ref, o_ref, l_ref, own_ref, recv_ref, *refs):
    n = len(chunks)
    if last:
        out_ref, keys, turned, values, mask, sems = refs
    else:
        out_ref, newl_ref, keys, turned, values, mask, sems = refs
    g = pl.program_id(0)
    core = at_ref[3]
    rows = 256
    swap = {1: 2, 2: 1}
    cuts = [slice(j * HD, (j + 1) * HD) for j in range(HEADS)]

    def fetch(k_ref, v_ref):
        copies = [pltpu.make_async_copy(k_ref, keys, sems.at[n])]
        for i, t in enumerate(chunks):
            j = chunks.index(swap.get(t, t))
            copies.append(
                pltpu.make_async_copy(
                    v_ref.at[pl.ds(j * rows, rows), :], turned.at[pl.ds(i * rows, rows), :], sems.at[i]
                )
            )
        for copy in copies:
            copy.start()
        for copy in copies:
            copy.wait()

    @pl.when((g == 0) & (core == 0))
    def _():
        fetch(own_ref, recv_ref)

    @pl.when((g == 0) & (core == 1))
    def _():
        fetch(recv_ref, own_ref)

    @pl.when(g == 0)
    def _():
        same = eye(HD)
        for i in range(n):
            to = slice(i * rows, (i + 1) * rows)
            for h in range(HEADS):
                values[h, :HD, to] = dot(same, turned[to, cuts[h]], NT).astype(bf16)
        values[:, HD:, :] = jnp.ones((HEADS, 16, n * rows), bf16)
        x, y = at_ref[0], at_ref[1]
        lane = lax.broadcasted_iota(jnp.int32, (rows, HD), 1)
        offsets = jnp.zeros((rows, HD), jnp.int32)
        for e in range(8):
            offsets = jnp.where(lane == e, off_ref[e], offsets)
        r = lax.broadcasted_iota(jnp.int32, (rows, HD), 0)
        part, inside = r // 64, ((r // 16) % 2) * 4 + ((r // 32) % 2) * 2 + (r % 16) // SLOTS
        for i, t in enumerate(chunks):
            demo = (((x - part) & 3) * 4 + ((y + STEP[t]) & 3)) * 8 + inside
            mask[i * rows : (i + 1) * rows, :] = jnp.where(demo < offsets, 0.0, NEG).astype(bf16)

    lane = lax.broadcasted_iota(jnp.int32, (group * QLEN, HD), 1)
    row = lax.broadcasted_iota(jnp.int32, (group * QLEN, HD), 0)
    which = (lane == group * g + row // QLEN).astype(f32).astype(bf16)

    def score(j):
        k = jnp.concatenate([keys[:, cuts[j]], mask[...]], axis=1)
        return dot(k, jnp.concatenate([q_ref[:, cuts[j]], which], axis=1), NT)

    def weigh(j, s):
        before = l_ref[0, j : j + 1, :]
        top = jnp.maximum(jnp.max(s, 0, keepdims=True) * EXPO, before)
        return top, jnp.exp2(before - top), jnp.exp2(s * EXPO - top).astype(bf16)

    def finish(j, top, w, p):
        r = dot(values[j], p)
        den = r[HD : HD + 1, :] + w
        res = (o_ref[0, cuts[j], :].astype(f32) * w + r[:HD, :]) * (1.0 / den)
        if last:
            out_ref[:, cuts[j]] = jnp.transpose(res).astype(bf16)
        else:
            out_ref[0, cuts[j], :] = res.astype(bf16)
            newl_ref[0, j : j + 1, :] = top + jnp.log2(den)

    scores = [score(j) for j in range(ahead)]
    ready = []
    for j in range(HEADS):
        if j + ahead < HEADS:
            scores.append(score(j + ahead))
        ready.append(weigh(j, scores[j]))
        if j >= ahead:
            finish(j - ahead, *ready[j - ahead])
    for j in range(HEADS - ahead, HEADS):
        finish(j, *ready[j])


def far_attention(at, offsets, q, state, own, recv, chunks, last, group=2, ahead=1):
    n = len(chunks)
    outs, specs = (shape(q.shape), query_spec(group)) if last else (state_shapes(q, group), state_specs(group))
    return pl.pallas_call(
        functools.partial(far_kernel, chunks, last, group, ahead),
        out_shape=outs,
        grid=(q.shape[0] // (group * QLEN),),
        in_specs=[SM, SM, query_spec(group), *state_specs(group), ANY, ANY],
        out_specs=specs,
        scratch_shapes=[
            pltpu.VMEM((n * 256, WIDTH), bf16),
            pltpu.VMEM((n * 256, WIDTH), bf16),
            pltpu.VMEM((HEADS, HD + 16, n * 256), bf16),
            pltpu.VMEM((n * 256, HD), bf16),
            pltpu.SemaphoreType.DMA((n + 1,)),
        ],
        cost_estimate=LARGE,
        compiler_params=pltpu.CompilerParams(vmem_limit_bytes=24 << 20),
    )(at, offsets, q, *state, own, recv)


def per_device(
    summary_states,
    summary_queries,
    summary_keys,
    summary_values,
    demo_keys,
    demo_values,
    demo_lengths,
    out_weight,
    norm_gain,
    key_weight,
    value_weight,
    query_queries,
    query_keys,
    query_values,
    query_offsets,
):
    shot = lax.axis_index("shot")
    head = lax.axis_index("head")
    x, y, z, c = shot >> 4, (shot >> 2) & 3, (shot >> 1) & 1, shot & 1
    at = jnp.stack([x, y, z, c, head]).astype(jnp.int32)
    core0 = c == 0

    out_t = out_weight.T
    out1, out2, pass_out = ring_y(out_t)
    kv = jnp.concatenate([key_weight, value_weight], axis=0)

    mine, give, gain_rows = demo_attention(
        demo_lengths, at, summary_queries, summary_keys, summary_values, demo_keys, demo_values, summary_states, norm_gain
    )
    theirs = send_z(after(give, out1, out2))
    out_parts = [out_t, out1, out2, pass_out(after(out1, give))]
    out_parts += [send_core(after(v, give)) for v in out_parts]
    pair = jnp.where(z == 0, jnp.concatenate([mine, theirs], axis=0), jnp.concatenate([theirs, mine], axis=0))
    rows = [pair] + [send_x(pair, k) for k in (1, 2, 3)]
    queries = query_queries, query_keys, query_values
    state = near_attention(after(at, pair), *queries, 0, 1)
    rows[0] = after(rows[0], state[1])


    own, give = call(out_kernel, (shape((144, HALF), f32), shape((144, HALF))), 13)(at, *rows, *out_parts, gain_rows)
    got = ring_head(give)
    kv1, kv2, pass_kv = ring_y(after(kv, give))
    kv_parts = [kv, kv1, kv2, pass_kv(after(kv1, got[0], got[1]))]
    kv_parts += [send_core(after(v, got[0], got[1])) for v in kv_parts[:3]] + [send_core(after(kv_parts[3], got[2]))]

    parts = call(project_kernel, (shape((32, WIDE), f32),) + (shape((32, WIDE)),) * 3, 12)(at, own, *got, *kv_parts)
    got = [send_x(parts[k], -k) for k in (1, 2, 3)]
    keep, give = call(half_kernel, (shape((32, WIDE), f32), shape((32, WIDE))), 4)(at, parts[0], *got)
    keep, give = call(compact_kernel, (shape((32, WIDTH)),) * 2, 2)(at, keep, send_z(give))
    got = send_core(give)

    row = jnp.where(core0, jnp.concatenate([keep, got], axis=0), jnp.concatenate([got, keep], axis=0))
    others = [send_x(row, k) for k in (1, 2, 3)]
    state = near_attention(after(at, row), *queries, 1, 3, state)
    plane = jnp.concatenate([after(row, state[1])] + others, axis=0)
    plane1, plane2, pass_plane = ring_y(plane)

    def far(state, chunks, *own):
        own = jnp.concatenate(own, axis=0)
        return far_attention(at, query_offsets, query_queries, state, own, send_core(own), chunks, chunks[-1] == 3)

    state = far(state, (0,), plane)
    plane3 = pass_plane(after(plane1, state[1]))
    state = far(state, (1, 2), after(plane1, state[1]), plane2)
    return far(state, (3,), after(plane3, state[1]))


def solution(mesh):
    return jax.shard_map(
        per_device,
        mesh=mesh,
        in_specs=(
            P("shot", "head"),
            P("shot", "head"),
            P("shot", "head"),
            P("shot", "head"),
            P("shot", None, "head"),
            P("shot", None, "head"),
            P("shot"),
            P("head", "shot"),
            P("head"),
            P("shot", "head"),
            P("shot", "head"),
            P("shot", "head"),
            P("shot", "head"),
            P("shot", "head"),
            P("shot"),
        ),
        out_specs=P("shot", "head"),
        check_vma=False,
    )
```

time: 689 us -> 122 us (0.18)
  waiting for transfers between devices: 530 us -> 33 us
  matrix products: 74.6 us -> 0 us
  starting transfers between devices: 0.38 us -> 45 us
  Pallas kernels: 0 us -> 39.7 us
  local copies, waits for them, and re-layouts: 31 us -> 3.13 us
  blocking collectives: 21.3 us -> 0 us
  other arithmetic: 16.1 us -> 0.92 us
  between operations: 13.7 us -> 0.42 us
    all_gather x5 -> x0, waiting for transfers between devices: 507 us -> none  [the longest x1 114 us: per_device(): lax.all_gather(out_weight, 'shot', axis=1, tiled=True)]
    dot_general x24 -> x0, matrix products: 74.6 us -> none  [the longest x8 35.1 us: one_head(): jnp.dot(weights.astype(jnp.bfloat16), vh, preferred_element_type=f32)]
    ppermute x0 -> x35, starting transfers between devices: none -> 45 us  [the longest x32 36.6 us: send(): lax.ppermute(v, 'shot', [(i, index(*to(*p))) for i, p in enumerate(places...]
    pallas_call x0 -> x10, Pallas kernels: none -> 39.7 us  [the longest x3 21.9 us: far_attention(): pl.pallas_call(functools.partial(far_kernel, chunks, last, group, ahead),...]
    ppermute x0 -> x35, waiting for transfers between devices: none -> 33 us  [the longest x32 23.2 us: send(): lax.ppermute(v, 'shot', [(i, index(*to(*p))) for i, p in enumerate(places...]
    reduce_scatter x1 -> x0, waiting for transfers between devices: 21 us -> none  [per_device(): lax.psum_scatter(partial_out, 'head', scatter_dimension=1, tiled=True)]
    while x16 -> x0, local copies, waits for them, and re-layouts: 15.3 us -> none
    all_gather x1 -> x0, blocking collectives: 11.2 us -> none  [per_device(): full_rows = lax.all_gather(normed, 'head', axis=1, tiled=True)]
  transfers between devices with their start and end apart: 6 -> 35, of which waited for: 6 -> 14; matrix products, arithmetic and copies ran while one was open for 5% -> 1% of each run, Pallas kernels for 0% -> 24%
where the time goes in v1:
time: 122 us
  starting transfers between devices  45 us (37%)
  Pallas kernels  39.7 us (33%)
  waiting for transfers between devices  33 us (27%)
  local copies, waits for them, and re-layouts  3.13 us (3%)
    ppermute x32, starting transfers between devices, send(): lax.ppermute(v, 'shot', [(i, index(*to(*p))) for i, p in enumerate(places...  36.6 us
    ppermute x32, waiting for transfers between devices, send(): lax.ppermute(v, 'shot', [(i, index(*to(*p))) for i, p in enumerate(places...  23.2 us
    pallas_call x3, Pallas kernels, far_attention(): pl.pallas_call(functools.partial(far_kernel, chunks, last, group, ahead),...  21.9 us
    ppermute x3, waiting for transfers between devices, step(): return lax.ppermute(u, ('shot', 'head'), pairs)  9.75 us
    pallas_call x2, Pallas kernels, near_attention(): pl.pallas_call(functools.partial(near_kernel, group), out_shape=state_sha...  8.82 us
    ppermute x3, starting transfers between devices, step(): return lax.ppermute(u, ('shot', 'head'), pairs)  8.36 us
    pallas_call x1, Pallas kernels, demo_attention(): pl.pallas_call(demo_kernel, out_shape=(shape((rows, WIDTH + HALF)), shape...  5.65 us
    unnamed x25, local copies, waits for them, and re-layouts  2.45 us
  transfers between devices with their start and end apart: 35, of which 14 were waited for; matrix products, arithmetic and copies ran while one was open for 1% of the time, Pallas kernels for 24%

profile of v1, /device:TPU:1, one launch (start us, length us, event | category | flops | bytes accessed | tf_op | source)
XLA Modules:
  0.0 122.1 jit_solution(8805970243558062564)
XLA Ops:
  0.0 2.1 %collective-permute-start.1 = (bf16[64,1024]{1,0:T(8,128)(2,1)}, bf16[64,1024]{1,0:T(8,128)(2,1)S(1)}, u32[]{:S(2)}, u32[]{:S(2)}) collective-permute-start(bf16[64,1024]{1,0:T(8,128)(2,1)} %bitcast.7), channel_id=1, source_target_pairs={{0,48},{4,20},{8,56},{12,28},{16,0},{20,36},{24,8},{28,44},{32,16}... | collective-permute-start | bytes 393224 | tf_op jit(solution)/shard_map/ppermute | solution.py:69
  2.1 1.4 %collective-permute-start = (bf16[64,1024]{1,0:T(8,128)(2,1)}, bf16[64,1024]{1,0:T(8,128)(2,1)S(1)}, u32[]{:S(2)}, u32[]{:S(2)}) collective-permute-start(bf16[64,1024]{1,0:T(8,128)(2,1)} %bitcast.8), channel_id=1, source_target_pairs={{0,16},{4,52},{8,24},{12,60},{16,32},{20,4},{24,40},{28,12},{32,48... | collective-permute-start | bytes 393224 | tf_op jit(solution)/shard_map/ppermute | solution.py:69
  4.2 5.7 %shard_map.145 = (bf16[16,1536]{1,0:T(8,128)(2,1)}, bf16[16,1536]{1,0:T(8,128)(2,1)}, bf16[16,512]{1,0:T(8,128)(2,1)}) custom-call(s32[2]{0:T(128)} %len_ref.1, s32[5]{0:T(128)} %stack.23.at_ref, bf16[16,1024]{1,0:T(8,128)(2,1)} %q_ref.6, bf16[16,1024]{1,0:T(8,128)(2,1)} %ks_ref.1, bf16[16,1024]{1,0:T(8,128)(2,1)} %vs_ref.1, bf16[2,512,1024]{2,1,0:T(8,128)(2,1)} %kc_ref.1, ...), custom_call_target="tpu_custom_call" | custom-call | flops 1000 | bytes 1000 | tf_op jit(solution)/shard_map/pallas_call | solution.py:185
  9.9 1.8 %collective-permute-start.7 = (bf16[64,1024]{1,0:T(8,128)(2,1)S(1)}, bf16[64,1024]{1,0:T(8,128)(2,1)S(1)}, u32[]{:S(2)}, u32[]{:S(2)}) collective-permute-start(bf16[64,1024]{1,0:T(8,128)(2,1)S(1)} %bitcast.9), channel_id=1, source_target_pairs={{0,4},{4,0},{8,12},{12,8},{16,20},{20,16},{24,28},{28,24},{32,36},... | collective-permute-start | bytes 393224 | tf_op jit(solution)/shard_map/ppermute | solution.py:69
  11.7 1.0 collective-permute-start.2
  13.1 3.0 %collective-permute-start.6 = (bf16[64,1024]{1,0:T(8,128)(2,1)S(1)}, bf16[64,1024]{1,0:T(8,128)(2,1)S(1)}, u32[]{:S(2)}, u32[]{:S(2)}) collective-permute-start(bf16[64,1024]{1,0:T(8,128)(2,1)S(1)} %collective-permute-done.refs_5_), channel_id=1, source_target_pairs={{0,16},{4,52},{8,24},{12,60},{16,32},{20,4},{24,40},{28,12},{32,48... | collective-permute-start | bytes 393224 | tf_op jit(solution)/shard_map/ppermute | solution.py:69
  16.0 0.9 maximum_select_fusion.1.refs_0_
  17.0 2.6 %collective-permute-start.5 = (bf16[32,1536]{1,0:T(8,128)(2,1)S(1)}, bf16[32,1536]{1,0:T(8,128)(2,1)S(1)}, u32[]{:S(2)}, u32[]{:S(2)}) collective-permute-start(bf16[32,1536]{1,0:T(8,128)(2,1)S(1)} %maximum_select_fusion.1.refs_0_), channel_id=1, source_target_pairs={{0,192},{4,196},{8,200},{12,204},{16,208},{20,212},{24,216},{28,22... | collective-permute-start | bytes 294920 | tf_op jit(solution)/shard_map/ppermute | solution.py:69
  19.5 1.2 collective-permute-start.4
  21.0 2.0 %collective-permute-start.10 = (bf16[64,1024]{1,0:T(8,128)(2,1)S(1)}, bf16[64,1024]{1,0:T(8,128)(2,1)S(1)}, u32[]{:S(2)}, u32[]{:S(2)}) collective-permute-start(bf16[64,1024]{1,0:T(8,128)(2,1)S(1)} %collective-permute-done.6.refs_7_), channel_id=1, source_target_pairs={{0,4},{4,0},{8,12},{12,8},{16,20},{20,16},{24,28},{28,24},{32,36},... | collective-permute-start | bytes 393224 | tf_op jit(solution)/shard_map/ppermute | solution.py:69
  23.1 3.1 %shard_map.146 = (bf16[4,1024,256]{2,1,0:T(8,128)(2,1)}, f32[4,8,256]{2,1,0:T(8,128)}) custom-call(s32[5]{0:T(128)} %stack.23.at_ref, bf16[1024,1024]{1,0:T(8,128)(2,1)} %q_ref.11, bf16[1024,1024]{1,0:T(8,128)(2,1)} %k_ref.3, bf16[1024,1024]{1,0:T(8,128)(2,1)} %v_ref.3), custom_call_target="tpu_custom_call" | custom-call | flops 49999998976 | bytes 1000 | tf_op jit(solution)/shard_map/pallas_call | solution.py:247
  26.7 1.0 shard_map.147
  27.7 3.4 %collective-permute-start.14 = (bf16[128,1024]{1,0:T(8,128)(2,1)S(1)}, bf16[128,1024]{1,0:T(8,128)(2,1)S(1)}, u32[]{:S(2)}, u32[]{:S(2)}) collective-permute-start(bf16[128,1024]{1,0:T(8,128)(2,1)S(1)} %constant_dynamic-update-slice_fusion.refs_0_), channel_id=1, source_target_pairs={{0,16},{4,52},{8,24},{12,60},{16,32},{20,4},{24,40},{28,12},{32,48... | collective-permute-start | bytes 786440 | tf_op jit(solution)/shard_map/ppermute | solution.py:69
  31.1 3.0 %collective-permute-start.12 = (bf16[144,512]{1,0:T(8,128)(2,1)S(1)}, bf16[144,512]{1,0:T(8,128)(2,1)S(1)}, u32[]{:S(2)}, u32[]{:S(2)}) collective-permute-start(bf16[144,512]{1,0:T(8,128)(2,1)S(1)} %get-tuple-element.54), channel_id=1, source_target_pairs={{0,3},{1,0},{2,1},{3,2},{4,5},{5,6},{6,7},{7,4},{8,11},{9,8},{10,9... | collective-permute-start | bytes 442376 | tf_op jit(solution)/shard_map/ppermute | solution.py:105
  34.1 2.6 %collective-permute-start.11 = (bf16[144,512]{1,0:T(8,128)(2,1)S(1)}, bf16[144,512]{1,0:T(8,128)(2,1)S(1)}, u32[]{:S(2)}, u32[]{:S(2)}) collective-permute-start(bf16[144,512]{1,0:T(8,128)(2,1)S(1)} %get-tuple-element.54), channel_id=1, source_target_pairs={{0,1},{1,2},{2,3},{3,0},{4,7},{5,4},{6,5},{7,6},{8,9},{9,10},{10,1... | collective-permute-start | bytes 442376 | tf_op jit(solution)/shard_map/ppermute | solution.py:105
  36.7 2.6 %collective-permute-done.12.b_ref = bf16[144,512]{1,0:T(8,128)(2,1)S(1)} collective-permute-done((bf16[144,512]{1,0:T(8,128)(2,1)S(1)}, bf16[144,512]{1,0:T(8,128)(2,1)S(1)}, u32[]{:S(2)}, u32[]{:S(2)}) %collective-permute-start.12) | collective-permute-done | bytes 147488 | tf_op jit(solution)/shard_map/ppermute | solution.py:105
  39.3 3.0 %collective-permute-done.11.a_ref = bf16[144,512]{1,0:T(8,128)(2,1)S(1)} collective-permute-done((bf16[144,512]{1,0:T(8,128)(2,1)S(1)}, bf16[144,512]{1,0:T(8,128)(2,1)S(1)}, u32[]{:S(2)}, u32[]{:S(2)}) %collective-permute-start.11) | collective-permute-done | bytes 147488 | tf_op jit(solution)/shard_map/ppermute | solution.py:105
  42.3 0.9 collective-permute-start.16
  43.2 2.8 %collective-permute-start.13 = (bf16[144,512]{1,0:T(8,128)(2,1)S(1)}, bf16[144,512]{1,0:T(8,128)(2,1)S(1)}, u32[]{:S(2)}, u32[]{:S(2)}) collective-permute-start(bf16[144,512]{1,0:T(8,128)(2,1)S(1)} %collective-permute-done.11.a_ref), channel_id=1, source_target_pairs={{0,1},{1,2},{2,3},{3,0},{4,7},{5,4},{6,5},{7,6},{8,9},{9,10},{10,1... | collective-permute-start | bytes 442376 | tf_op jit(solution)/shard_map/ppermute | solution.py:105
  46.6 4.2 %collective-permute-done.13.c_ref = bf16[144,512]{1,0:T(8,128)(2,1)S(1)} collective-permute-done((bf16[144,512]{1,0:T(8,128)(2,1)S(1)}, bf16[144,512]{1,0:T(8,128)(2,1)S(1)}, u32[]{:S(2)}, u32[]{:S(2)}) %collective-permute-start.13) | collective-permute-done | bytes 147488 | tf_op jit(solution)/shard_map/ppermute | solution.py:105
  50.8 3.1 %collective-permute-start.20 = (bf16[128,1024]{1,0:T(8,128)(2,1)S(1)}, bf16[128,1024]{1,0:T(8,128)(2,1)S(1)}, u32[]{:S(2)}, u32[]{:S(2)}) collective-permute-start(bf16[128,1024]{1,0:T(8,128)(2,1)S(1)} %collective-permute-done.16.refs_3_), channel_id=1, source_target_pairs={{0,4},{4,0},{8,12},{12,8},{16,20},{20,16},{24,28},{28,24},{32,36},... | collective-permute-start | bytes 786440 | tf_op jit(solution)/shard_map/ppermute | solution.py:69
  54.0 1.1 collective-permute-done.20.refs_7_
  55.1 1.0 shard_map.148
  56.3 1.4 %collective-permute-start.22 = (bf16[32,2176]{1,0:T(8,128)(2,1)S(1)}, bf16[32,2176]{1,0:T(8,128)(2,1)S(1)}, u32[]{:S(2)}, u32[]{:S(2)}) collective-permute-start(bf16[32,2176]{1,0:T(8,128)(2,1)S(1)} %get-tuple-element.62), channel_id=1, source_target_pairs={{0,128},{4,132},{8,136},{12,140},{16,144},{20,148},{24,152},{28,15... | collective-permute-start | bytes 417800 | tf_op jit(solution)/shard_map/ppermute | solution.py:69
  57.8 3.3 %collective-permute-done.21.a_ref = bf16[32,2176]{1,0:T(8,128)(2,1)S(1)} collective-permute-done((bf16[32,2176]{1,0:T(8,128)(2,1)S(1)}, bf16[32,2176]{1,0:T(8,128)(2,1)S(1)}, u32[]{:S(2)}, u32[]{:S(2)}) %collective-permute-start.21) | collective-permute-done | bytes 139296 | tf_op jit(solution)/shard_map/ppermute | solution.py:69
  61.1 1.3 %collective-permute-done.22.b_ref = bf16[32,2176]{1,0:T(8,128)(2,1)S(1)} collective-permute-done((bf16[32,2176]{1,0:T(8,128)(2,1)S(1)}, bf16[32,2176]{1,0:T(8,128)(2,1)S(1)}, u32[]{:S(2)}, u32[]{:S(2)}) %collective-permute-start.22) | collective-permute-done | bytes 139296 | tf_op jit(solution)/shard_map/ppermute | solution.py:69
  62.4 3.8 %collective-permute-done.23.c_ref = bf16[32,2176]{1,0:T(8,128)(2,1)S(1)} collective-permute-done((bf16[32,2176]{1,0:T(8,128)(2,1)S(1)}, bf16[32,2176]{1,0:T(8,128)(2,1)S(1)}, u32[]{:S(2)}, u32[]{:S(2)}) %collective-permute-start.23) | collective-permute-done | bytes 139296 | tf_op jit(solution)/shard_map/ppermute | solution.py:69
  66.2 0.6 shard_map.149
  66.8 1.5 %collective-permute-start.24 = (bf16[32,2176]{1,0:T(8,128)(2,1)S(1)}, bf16[32,2176]{1,0:T(8,128)(2,1)S(1)}, u32[]{:S(2)}, u32[]{:S(2)}) collective-permute-start(bf16[32,2176]{1,0:T(8,128)(2,1)S(1)} %get-tuple-element.65), channel_id=1, source_target_pairs={{0,8},{4,12},{8,0},{12,4},{16,24},{20,28},{24,16},{28,20},{32,40},... | collective-permute-start | bytes 417800 | tf_op jit(solution)/shard_map/ppermute | solution.py:69
  68.4 3.1 %collective-permute-done.24.a_ref = bf16[32,2176]{1,0:T(8,128)(2,1)S(1)} collective-permute-done((bf16[32,2176]{1,0:T(8,128)(2,1)S(1)}, bf16[32,2176]{1,0:T(8,128)(2,1)S(1)}, u32[]{:S(2)}, u32[]{:S(2)}) %collective-permute-start.24) | collective-permute-done | bytes 139296 | tf_op jit(solution)/shard_map/ppermute | solution.py:69
  71.4 0.6 shard_map.150
  72.1 1.7 %collective-permute-start.25 = (bf16[32,1024]{1,0:T(8,128)(2,1)S(1)}, bf16[32,1024]{1,0:T(8,128)(2,1)S(1)}, u32[]{:S(2)}, u32[]{:S(2)}) collective-permute-start(bf16[32,1024]{1,0:T(8,128)(2,1)S(1)} %get-tuple-element.67), channel_id=1, source_target_pairs={{0,4},{4,0},{8,12},{12,8},{16,20},{20,16},{24,28},{28,24},{32,36},... | collective-permute-start | bytes 196616 | tf_op jit(solution)/shard_map/ppermute | solution.py:69
  73.8 0.9 collective-permute-done.25
  75.2 1.3 %collective-permute-start.27 = (bf16[64,1024]{1,0:T(8,128)(2,1)S(1)}, bf16[64,1024]{1,0:T(8,128)(2,1)S(1)}, u32[]{:S(2)}, u32[]{:S(2)}) collective-permute-start(bf16[64,1024]{1,0:T(8,128)(2,1)S(1)} %maximum_select_fusion), channel_id=1, source_target_pairs={{0,128},{4,132},{8,136},{12,140},{16,144},{20,148},{24,152},{28,15... | collective-permute-start | bytes 393224 | tf_op jit(solution)/shard_map/ppermute | solution.py:69
  76.5 0.8 collective-permute-start.26
  77.3 5.7 %shard_map.151 = (bf16[4,1024,256]{2,1,0:T(8,128)(2,1)}, f32[4,8,256]{2,1,0:T(8,128)}) custom-call(s32[5]{0:T(128)} %stack.23.at_ref, bf16[1024,1024]{1,0:T(8,128)(2,1)} %q_ref.11, bf16[1024,1024]{1,0:T(8,128)(2,1)} %k_ref.3, bf16[1024,1024]{1,0:T(8,128)(2,1)} %v_ref.3, ...), custom_call_target="tpu_custom_call", output_to_operand_aliasing={{0}: (4, {}), {1}: (5, {})} | custom-call | flops 49999998976 | bytes 1000 | tf_op jit(solution)/shard_map/pallas_call | solution.py:247
  83.0 1.8 %collective-permute-done.26 = bf16[64,1024]{1,0:T(8,128)(2,1)S(1)} collective-permute-done((bf16[64,1024]{1,0:T(8,128)(2,1)S(1)}, bf16[64,1024]{1,0:T(8,128)(2,1)S(1)}, u32[]{:S(2)}, u32[]{:S(2)}) %collective-permute-start.26) | collective-permute-done | bytes 131104 | tf_op jit(solution)/shard_map/ppermute | solution.py:69
  84.9 0.7 collective-permute-start.29
  85.6 2.4 %collective-permute-start.31 = (bf16[256,1024]{1,0:T(8,128)(2,1)S(1)}, bf16[256,1024]{1,0:T(8,128)(2,1)S(1)}, u32[]{:S(2)}, u32[]{:S(2)}) collective-permute-start(bf16[256,1024]{1,0:T(8,128)(2,1)S(1)} %constant_dynamic-update-slice_fusion.2.own_ref), channel_id=1, source_target_pairs={{0,48},{4,20},{8,56},{12,28},{16,0},{20,36},{24,8},{28,44},{32,16}... | collective-permute-start | bytes 1572872 | tf_op jit(solution)/shard_map/ppermute | solution.py:69
  88.3 1.6 %copy-done.6 = bf16[4,1024,256]{2,1,0:T(8,128)(2,1)S(1)} copy-done((bf16[4,1024,256]{2,1,0:T(8,128)(2,1)S(1)}, bf16[4,1024,256]{2,1,0:T(8,128)(2,1)}, u32[]{:S(2)}) %copy-start.6) | copy-done | bytes 2097176
  89.9 0.8 copy-done.7
  90.6 5.6 %shard_map.152 = (bf16[4,1024,256]{2,1,0:T(8,128)(2,1)S(1)}, f32[4,8,256]{2,1,0:T(8,128)S(1)}) custom-call(s32[5]{0:T(128)S(1)} %copy-done.2, s32[8]{0:T(128)S(1)} %copy-done.5, bf16[1024,1024]{1,0:T(8,128)(2,1)S(1)} %copy-done.4, bf16[4,1024,256]{2,1,0:T(8,128)(2,1)S(1)} %copy-done.6, f32[4,8,256]{2,1,0:T(8,128)S(1)} %copy-done.7, ...), custom_call_target="tpu_custom_call" | custom-call | flops 49999998976 | bytes 1000 | tf_op jit(solution)/shard_map/pallas_call | solution.py:414
  96.2 4.5 %collective-permute-done.30 = bf16[256,1024]{1,0:T(8,128)(2,1)S(1)} collective-permute-done((bf16[256,1024]{1,0:T(8,128)(2,1)S(1)}, bf16[256,1024]{1,0:T(8,128)(2,1)S(1)}, u32[]{:S(2)}, u32[]{:S(2)}) %collective-permute-start.30) | collective-permute-done | bytes 524320 | tf_op jit(solution)/shard_map/ppermute | solution.py:69
  101.3 1.0 collective-permute-start.33
  102.3 1.3 %collective-permute-done.32.recv_ref = bf16[512,1024]{1,0:T(8,128)(2,1)S(1)} collective-permute-done((bf16[512,1024]{1,0:T(8,128)(2,1)S(1)}, bf16[512,1024]{1,0:T(8,128)(2,1)S(1)}, u32[]{:S(2)}, u32[]{:S(2)}) %collective-permute-start.32) | collective-permute-done | bytes 1048608 | tf_op jit(solution)/shard_map/ppermute | solution.py:69
  103.6 9.2 %shard_map.153 = (bf16[4,1024,256]{2,1,0:T(8,128)(2,1)S(1)}, f32[4,8,256]{2,1,0:T(8,128)S(1)}) custom-call(s32[5]{0:T(128)S(1)} %copy-done.2, s32[8]{0:T(128)S(1)} %copy-done.5, bf16[1024,1024]{1,0:T(8,128)(2,1)S(1)} %copy-done.4, bf16[4,1024,256]{2,1,0:T(8,128)(2,1)S(1)} %get-tuple-element.73.o_ref, f32[4,8,256]{2,1,0:T(8,128)S(1)} %get-tuple-element.74.l_ref, ...), custom_call_target="tpu_custom_call" | custom-call | flops 49999998976 | bytes 1000 | tf_op jit(solution)/shard_map/pallas_call | solution.py:414
  113.2 1.5 %collective-permute-done.34.recv_ref = bf16[256,1024]{1,0:T(8,128)(2,1)S(1)} collective-permute-done((bf16[256,1024]{1,0:T(8,128)(2,1)S(1)}, bf16[256,1024]{1,0:T(8,128)(2,1)S(1)}, u32[]{:S(2)}, u32[]{:S(2)}) %collective-permute-start.34) | collective-permute-done | bytes 524320 | tf_op jit(solution)/shard_map/ppermute | solution.py:69
  114.8 7.1 %shard_map.154 = bf16[1024,1024]{1,0:T(8,128)(2,1)} custom-call(s32[5]{0:T(128)S(1)} %copy-done.2, s32[8]{0:T(128)S(1)} %copy-done.5, bf16[1024,1024]{1,0:T(8,128)(2,1)S(1)} %copy-done.4, bf16[4,1024,256]{2,1,0:T(8,128)(2,1)S(1)} %get-tuple-element.76.o_ref, f32[4,8,256]{2,1,0:T(8,128)S(1)} %get-tuple-element.77.l_ref, ...), custom_call_target="tpu_custom_call" | custom-call | flops 49999998976 | bytes 1000 | tf_op jit(solution)/shard_map/pallas_call | solution.py:414
  (63 shorter events, 4.6 us)
Async XLA Ops:
  0.0 11.7 %collective-permute-start.1 = (bf16[64,1024]{1,0:T(8,128)(2,1)}, bf16[64,1024]{1,0:T(8,128)(2,1)S(1)}, u32[]{:S(2)}, u32[]{:S(2)}) collective-permute-start(bf16[64,1024]{1,0:T(8,128)(2,1)} %bitcast.7), channel_id=1, source_target_pairs={{0,48},{4,20},{8,56},{12,28},{16,0},{20,36},{24,8},{28,44},{32,16}... | collective-permute-start | bytes 393224 | tf_op jit(solution)/shard_map/ppermute | solution.py:69
  2.1 9.6 %collective-permute-start = (bf16[64,1024]{1,0:T(8,128)(2,1)}, bf16[64,1024]{1,0:T(8,128)(2,1)S(1)}, u32[]{:S(2)}, u32[]{:S(2)}) collective-permute-start(bf16[64,1024]{1,0:T(8,128)(2,1)} %bitcast.8), channel_id=1, source_target_pairs={{0,16},{4,52},{8,24},{12,60},{16,32},{20,4},{24,40},{28,12},{32,48... | collective-permute-start | bytes 393224 | tf_op jit(solution)/shard_map/ppermute | solution.py:69
  4.2 5.7 %copy-start = (bf16[1024,64]{0,1:T(8,128)(2,1)S(1)}, bf16[1024,64]{0,1:T(8,128)(2,1)}, u32[]{:S(2)}) copy-start(bf16[1024,64]{0,1:T(8,128)(2,1)} %param.22) | copy-start | bytes 393220
  4.2 7.5 %copy-start.8 = (bf16[64,1024]{1,0:T(8,128)(2,1)S(1)}, bf16[64,1024]{1,0:T(8,128)(2,1)}, u32[]{:S(2)}) copy-start(bf16[64,1024]{1,0:T(8,128)(2,1)} %param.24) | copy-start | bytes 393220
  4.2 8.5 %copy-start.9 = (bf16[64,1024]{1,0:T(8,128)(2,1)S(1)}, bf16[64,1024]{1,0:T(8,128)(2,1)}, u32[]{:S(2)}) copy-start(bf16[64,1024]{1,0:T(8,128)(2,1)} %param.25) | copy-start | bytes 393220
  9.9 10.9 %collective-permute-start.7 = (bf16[64,1024]{1,0:T(8,128)(2,1)S(1)}, bf16[64,1024]{1,0:T(8,128)(2,1)S(1)}, u32[]{:S(2)}, u32[]{:S(2)}) collective-permute-start(bf16[64,1024]{1,0:T(8,128)(2,1)S(1)} %bitcast.9), channel_id=1, source_target_pairs={{0,4},{4,0},{8,12},{12,8},{16,20},{20,16},{24,28},{28,24},{32,36},... | collective-permute-start | bytes 393224 | tf_op jit(solution)/shard_map/ppermute | solution.py:69
  11.7 4.4 %collective-permute-start.2 = (bf16[16,1536]{1,0:T(8,128)(2,1)}, bf16[16,1536]{1,0:T(8,128)(2,1)S(1)}, u32[]{:S(2)}, u32[]{:S(2)}) collective-permute-start(bf16[16,1536]{1,0:T(8,128)(2,1)} %get-tuple-element.44), channel_id=1, source_target_pairs={{0,8},{4,12},{8,0},{12,4},{16,24},{20,28},{24,16},{28,20},{32,40},... | collective-permute-start | bytes 147464 | tf_op jit(solution)/shard_map/ppermute | solution.py:69
  12.7 13.5 %collective-permute-start.8 = (bf16[64,1024]{1,0:T(8,128)(2,1)S(1)}, bf16[64,1024]{1,0:T(8,128)(2,1)S(1)}, u32[]{:S(2)}, u32[]{:S(2)}) collective-permute-start(bf16[64,1024]{1,0:T(8,128)(2,1)S(1)} %collective-permute-done.refs_5_), channel_id=1, source_target_pairs={{0,4},{4,0},{8,12},{12,8},{16,20},{20,16},{24,28},{28,24},{32,36},... | collective-permute-start | bytes 393224 | tf_op jit(solution)/shard_map/ppermute | solution.py:69
  13.1 6.4 %collective-permute-start.6 = (bf16[64,1024]{1,0:T(8,128)(2,1)S(1)}, bf16[64,1024]{1,0:T(8,128)(2,1)S(1)}, u32[]{:S(2)}, u32[]{:S(2)}) collective-permute-start(bf16[64,1024]{1,0:T(8,128)(2,1)S(1)} %collective-permute-done.refs_5_), channel_id=1, source_target_pairs={{0,16},{4,52},{8,24},{12,60},{16,32},{20,4},{24,40},{28,12},{32,48... | collective-permute-start | bytes 393224 | tf_op jit(solution)/shard_map/ppermute | solution.py:69
  16.0 5.0 %collective-permute-start.9 = (bf16[64,1024]{1,0:T(8,128)(2,1)S(1)}, bf16[64,1024]{1,0:T(8,128)(2,1)S(1)}, u32[]{:S(2)}, u32[]{:S(2)}) collective-permute-start(bf16[64,1024]{1,0:T(8,128)(2,1)S(1)} %collective-permute-done.1.refs_6_), channel_id=1, source_target_pairs={{0,4},{4,0},{8,12},{12,8},{16,20},{20,16},{24,28},{28,24},{32,36},... | collective-permute-start | bytes 393224 | tf_op jit(solution)/shard_map/ppermute | solution.py:69
  16.9 9.7 %copy-start.1 = (s32[5]{0:T(128)S(1)}, s32[5]{0:T(128)}, u32[]{:S(2)}) copy-start(s32[5]{0:T(128)} %stack.23.at_ref) | copy-start | bytes 64
  16.9 9.7 %copy-start.3 = (bf16[16,512]{1,0:T(8,128)(2,1)S(1)}, bf16[16,512]{1,0:T(8,128)(2,1)}, u32[]{:S(2)}) copy-start(bf16[16,512]{1,0:T(8,128)(2,1)} %get-tuple-element.52.refs_12_) | copy-start | bytes 49156
  17.0 9.2 %collective-permute-start.5 = (bf16[32,1536]{1,0:T(8,128)(2,1)S(1)}, bf16[32,1536]{1,0:T(8,128)(2,1)S(1)}, u32[]{:S(2)}, u32[]{:S(2)}) collective-permute-start(bf16[32,1536]{1,0:T(8,128)(2,1)S(1)} %maximum_select_fusion.1.refs_0_), channel_id=1, source_target_pairs={{0,192},{4,196},{8,200},{12,204},{16,208},{20,212},{24,216},{28,22... | collective-permute-start | bytes 294920 | tf_op jit(solution)/shard_map/ppermute | solution.py:69
  19.5 6.7 %collective-permute-start.4 = (bf16[32,1536]{1,0:T(8,128)(2,1)S(1)}, bf16[32,1536]{1,0:T(8,128)(2,1)S(1)}, u32[]{:S(2)}, u32[]{:S(2)}) collective-permute-start(bf16[32,1536]{1,0:T(8,128)(2,1)S(1)} %maximum_select_fusion.1.refs_0_), channel_id=1, source_target_pairs={{0,128},{4,132},{8,136},{12,140},{16,144},{20,148},{24,152},{28,15... | collective-permute-start | bytes 294920 | tf_op jit(solution)/shard_map/ppermute | solution.py:69
  20.7 5.9 %collective-permute-start.3 = (bf16[32,1536]{1,0:T(8,128)(2,1)S(1)}, bf16[32,1536]{1,0:T(8,128)(2,1)S(1)}, u32[]{:S(2)}, u32[]{:S(2)}) collective-permute-start(bf16[32,1536]{1,0:T(8,128)(2,1)S(1)} %maximum_select_fusion.1.refs_0_), channel_id=1, source_target_pairs={{0,64},{4,68},{8,72},{12,76},{16,80},{20,84},{24,88},{28,92},{32,9... | collective-permute-start | bytes 294920 | tf_op jit(solution)/shard_map/ppermute | solution.py:69
  21.0 5.6 %collective-permute-start.10 = (bf16[64,1024]{1,0:T(8,128)(2,1)S(1)}, bf16[64,1024]{1,0:T(8,128)(2,1)S(1)}, u32[]{:S(2)}, u32[]{:S(2)}) collective-permute-start(bf16[64,1024]{1,0:T(8,128)(2,1)S(1)} %collective-permute-done.6.refs_7_), channel_id=1, source_target_pairs={{0,4},{4,0},{8,12},{12,8},{16,20},{20,16},{24,28},{28,24},{32,36},... | collective-permute-start | bytes 393224 | tf_op jit(solution)/shard_map/ppermute | solution.py:69
  27.7 14.6 %collective-permute-start.14 = (bf16[128,1024]{1,0:T(8,128)(2,1)S(1)}, bf16[128,1024]{1,0:T(8,128)(2,1)S(1)}, u32[]{:S(2)}, u32[]{:S(2)}) collective-permute-start(bf16[128,1024]{1,0:T(8,128)(2,1)S(1)} %constant_dynamic-update-slice_fusion.refs_0_), channel_id=1, source_target_pairs={{0,16},{4,52},{8,24},{12,60},{16,32},{20,4},{24,40},{28,12},{32,48... | collective-permute-start | bytes 786440 | tf_op jit(solution)/shard_map/ppermute | solution.py:69
  31.1 8.2 %collective-permute-start.12 = (bf16[144,512]{1,0:T(8,128)(2,1)S(1)}, bf16[144,512]{1,0:T(8,128)(2,1)S(1)}, u32[]{:S(2)}, u32[]{:S(2)}) collective-permute-start(bf16[144,512]{1,0:T(8,128)(2,1)S(1)} %get-tuple-element.54), channel_id=1, source_target_pairs={{0,3},{1,0},{2,1},{3,2},{4,5},{5,6},{6,7},{7,4},{8,11},{9,8},{10,9... | collective-permute-start | bytes 442376 | tf_op jit(solution)/shard_map/ppermute | solution.py:105
  34.1 8.2 %collective-permute-start.11 = (bf16[144,512]{1,0:T(8,128)(2,1)S(1)}, bf16[144,512]{1,0:T(8,128)(2,1)S(1)}, u32[]{:S(2)}, u32[]{:S(2)}) collective-permute-start(bf16[144,512]{1,0:T(8,128)(2,1)S(1)} %get-tuple-element.54), channel_id=1, source_target_pairs={{0,1},{1,2},{2,3},{3,0},{4,7},{5,4},{6,5},{7,6},{8,9},{9,10},{10,1... | collective-permute-start | bytes 442376 | tf_op jit(solution)/shard_map/ppermute | solution.py:105
  36.7 9.8 %collective-permute-start.15 = (bf16[128,1024]{1,0:T(8,128)(2,1)S(1)}, bf16[128,1024]{1,0:T(8,128)(2,1)S(1)}, u32[]{:S(2)}, u32[]{:S(2)}) collective-permute-start(bf16[128,1024]{1,0:T(8,128)(2,1)S(1)} %constant_dynamic-update-slice_fusion.refs_0_), channel_id=1, source_target_pairs={{0,48},{4,20},{8,56},{12,28},{16,0},{20,36},{24,8},{28,44},{32,16}... | collective-permute-start | bytes 786440 | tf_op jit(solution)/shard_map/ppermute | solution.py:69
  42.3 8.5 %collective-permute-start.16 = (bf16[128,1024]{1,0:T(8,128)(2,1)S(1)}, bf16[128,1024]{1,0:T(8,128)(2,1)S(1)}, u32[]{:S(2)}, u32[]{:S(2)}) collective-permute-start(bf16[128,1024]{1,0:T(8,128)(2,1)S(1)} %collective-permute-done.14.refs_1_), channel_id=1, source_target_pairs={{0,16},{4,52},{8,24},{12,60},{16,32},{20,4},{24,40},{28,12},{32,48... | collective-permute-start | bytes 786440 | tf_op jit(solution)/shard_map/ppermute | solution.py:69
  43.2 7.6 %collective-permute-start.13 = (bf16[144,512]{1,0:T(8,128)(2,1)S(1)}, bf16[144,512]{1,0:T(8,128)(2,1)S(1)}, u32[]{:S(2)}, u32[]{:S(2)}) collective-permute-start(bf16[144,512]{1,0:T(8,128)(2,1)S(1)} %collective-permute-done.11.a_ref), channel_id=1, source_target_pairs={{0,1},{1,2},{2,3},{3,0},{4,7},{5,4},{6,5},{7,6},{8,9},{9,10},{10,1... | collective-permute-start | bytes 442376 | tf_op jit(solution)/shard_map/ppermute | solution.py:105
  46.0 8.0 %collective-permute-start.17 = (bf16[128,1024]{1,0:T(8,128)(2,1)S(1)}, bf16[128,1024]{1,0:T(8,128)(2,1)S(1)}, u32[]{:S(2)}, u32[]{:S(2)}) collective-permute-start(bf16[128,1024]{1,0:T(8,128)(2,1)S(1)} %constant_dynamic-update-slice_fusion.refs_0_), channel_id=1, source_target_pairs={{0,4},{4,0},{8,12},{12,8},{16,20},{20,16},{24,28},{28,24},{32,36},... | collective-permute-start | bytes 786440 | tf_op jit(solution)/shard_map/ppermute | solution.py:69
  46.1 7.8 %collective-permute-start.18 = (bf16[128,1024]{1,0:T(8,128)(2,1)S(1)}, bf16[128,1024]{1,0:T(8,128)(2,1)S(1)}, u32[]{:S(2)}, u32[]{:S(2)}) collective-permute-start(bf16[128,1024]{1,0:T(8,128)(2,1)S(1)} %collective-permute-done.14.refs_1_), channel_id=1, source_target_pairs={{0,4},{4,0},{8,12},{12,8},{16,20},{20,16},{24,28},{28,24},{32,36},... | collective-permute-start | bytes 786440 | tf_op jit(solution)/shard_map/ppermute | solution.py:69
  46.5 7.4 %collective-permute-start.19 = (bf16[128,1024]{1,0:T(8,128)(2,1)S(1)}, bf16[128,1024]{1,0:T(8,128)(2,1)S(1)}, u32[]{:S(2)}, u32[]{:S(2)}) collective-permute-start(bf16[128,1024]{1,0:T(8,128)(2,1)S(1)} %collective-permute-done.15.refs_2_), channel_id=1, source_target_pairs={{0,4},{4,0},{8,12},{12,8},{16,20},{20,16},{24,28},{28,24},{32,36},... | collective-permute-start | bytes 786440 | tf_op jit(solution)/shard_map/ppermute | solution.py:69
  50.8 4.3 %collective-permute-start.20 = (bf16[128,1024]{1,0:T(8,128)(2,1)S(1)}, bf16[128,1024]{1,0:T(8,128)(2,1)S(1)}, u32[]{:S(2)}, u32[]{:S(2)}) collective-permute-start(bf16[128,1024]{1,0:T(8,128)(2,1)S(1)} %collective-permute-done.16.refs_3_), channel_id=1, source_target_pairs={{0,4},{4,0},{8,12},{12,8},{16,20},{20,16},{24,28},{28,24},{32,36},... | collective-permute-start | bytes 786440 | tf_op jit(solution)/shard_map/ppermute | solution.py:69
  56.1 5.0 %collective-permute-start.21 = (bf16[32,2176]{1,0:T(8,128)(2,1)S(1)}, bf16[32,2176]{1,0:T(8,128)(2,1)S(1)}, u32[]{:S(2)}, u32[]{:S(2)}) collective-permute-start(bf16[32,2176]{1,0:T(8,128)(2,1)S(1)} %get-tuple-element.61), channel_id=1, source_target_pairs={{0,192},{4,196},{8,200},{12,204},{16,208},{20,212},{24,216},{28,22... | collective-permute-start | bytes 417800 | tf_op jit(solution)/shard_map/ppermute | solution.py:69
  56.3 6.1 %collective-permute-start.22 = (bf16[32,2176]{1,0:T(8,128)(2,1)S(1)}, bf16[32,2176]{1,0:T(8,128)(2,1)S(1)}, u32[]{:S(2)}, u32[]{:S(2)}) collective-permute-start(bf16[32,2176]{1,0:T(8,128)(2,1)S(1)} %get-tuple-element.62), channel_id=1, source_target_pairs={{0,128},{4,132},{8,136},{12,140},{16,144},{20,148},{24,152},{28,15... | collective-permute-start | bytes 417800 | tf_op jit(solution)/shard_map/ppermute | solution.py:69
  57.8 8.4 %collective-permute-start.23 = (bf16[32,2176]{1,0:T(8,128)(2,1)S(1)}, bf16[32,2176]{1,0:T(8,128)(2,1)S(1)}, u32[]{:S(2)}, u32[]{:S(2)}) collective-permute-start(bf16[32,2176]{1,0:T(8,128)(2,1)S(1)} %get-tuple-element.63), channel_id=1, source_target_pairs={{0,64},{4,68},{8,72},{12,76},{16,80},{20,84},{24,88},{28,92},{32,9... | collective-permute-start | bytes 417800 | tf_op jit(solution)/shard_map/ppermute | solution.py:69
  66.8 4.6 %collective-permute-start.24 = (bf16[32,2176]{1,0:T(8,128)(2,1)S(1)}, bf16[32,2176]{1,0:T(8,128)(2,1)S(1)}, u32[]{:S(2)}, u32[]{:S(2)}) collective-permute-start(bf16[32,2176]{1,0:T(8,128)(2,1)S(1)} %get-tuple-element.65), channel_id=1, source_target_pairs={{0,8},{4,12},{8,0},{12,4},{16,24},{20,28},{24,16},{28,20},{32,40},... | collective-permute-start | bytes 417800 | tf_op jit(solution)/shard_map/ppermute | solution.py:69
  72.1 2.6 %collective-permute-start.25 = (bf16[32,1024]{1,0:T(8,128)(2,1)S(1)}, bf16[32,1024]{1,0:T(8,128)(2,1)S(1)}, u32[]{:S(2)}, u32[]{:S(2)}) collective-permute-start(bf16[32,1024]{1,0:T(8,128)(2,1)S(1)} %get-tuple-element.67), channel_id=1, source_target_pairs={{0,4},{4,0},{8,12},{12,8},{16,20},{20,16},{24,28},{28,24},{32,36},... | collective-permute-start | bytes 196616 | tf_op jit(solution)/shard_map/ppermute | solution.py:69
  74.7 10.2 %collective-permute-start.28 = (bf16[64,1024]{1,0:T(8,128)(2,1)S(1)}, bf16[64,1024]{1,0:T(8,128)(2,1)S(1)}, u32[]{:S(2)}, u32[]{:S(2)}) collective-permute-start(bf16[64,1024]{1,0:T(8,128)(2,1)S(1)} %maximum_select_fusion), channel_id=1, source_target_pairs={{0,192},{4,196},{8,200},{12,204},{16,208},{20,212},{24,216},{28,22... | collective-permute-start | bytes 393224 | tf_op jit(solution)/shard_map/ppermute | solution.py:69
  75.2 9.6 %collective-permute-start.27 = (bf16[64,1024]{1,0:T(8,128)(2,1)S(1)}, bf16[64,1024]{1,0:T(8,128)(2,1)S(1)}, u32[]{:S(2)}, u32[]{:S(2)}) collective-permute-start(bf16[64,1024]{1,0:T(8,128)(2,1)S(1)} %maximum_select_fusion), channel_id=1, source_target_pairs={{0,128},{4,132},{8,136},{12,140},{16,144},{20,148},{24,152},{28,15... | collective-permute-start | bytes 393224 | tf_op jit(solution)/shard_map/ppermute | solution.py:69
  76.5 8.3 %collective-permute-start.26 = (bf16[64,1024]{1,0:T(8,128)(2,1)S(1)}, bf16[64,1024]{1,0:T(8,128)(2,1)S(1)}, u32[]{:S(2)}, u32[]{:S(2)}) collective-permute-start(bf16[64,1024]{1,0:T(8,128)(2,1)S(1)} %maximum_select_fusion), channel_id=1, source_target_pairs={{0,64},{4,68},{8,72},{12,76},{16,80},{20,84},{24,88},{28,92},{32,9... | collective-permute-start | bytes 393224 | tf_op jit(solution)/shard_map/ppermute | solution.py:69
  77.3 11.0 %copy-start.2 = (s32[5]{0:T(128)S(1)}, s32[5]{0:T(128)}, u32[]{:S(2)}) copy-start(s32[5]{0:T(128)} %stack.23.at_ref) | copy-start | bytes 64
  77.3 11.0 %copy-start.4 = (bf16[1024,1024]{1,0:T(8,128)(2,1)S(1)}, bf16[1024,1024]{1,0:T(8,128)(2,1)}, u32[]{:S(2)}) copy-start(bf16[1024,1024]{1,0:T(8,128)(2,1)} %q_ref.11) | copy-start | bytes 6291460
  77.3 11.0 %copy-start.5 = (s32[8]{0:T(128)S(1)}, s32[8]{0:T(128)}, u32[]{:S(2)}) copy-start(s32[8]{0:T(128)} %off_ref.5) | copy-start | bytes 100
  84.9 3.4 %collective-permute-start.29 = (bf16[256,1024]{1,0:T(8,128)(2,1)S(1)}, bf16[256,1024]{1,0:T(8,128)(2,1)S(1)}, u32[]{:S(2)}, u32[]{:S(2)}) collective-permute-start(bf16[256,1024]{1,0:T(8,128)(2,1)S(1)} %constant_dynamic-update-slice_fusion.2.own_ref), channel_id=1, source_target_pairs={{0,4},{4,0},{8,12},{12,8},{16,20},{20,16},{24,28},{28,24},{32,36},... | collective-permute-start | bytes 1572872 | tf_op jit(solution)/shard_map/ppermute | solution.py:69
  85.6 15.2 %collective-permute-start.31 = (bf16[256,1024]{1,0:T(8,128)(2,1)S(1)}, bf16[256,1024]{1,0:T(8,128)(2,1)S(1)}, u32[]{:S(2)}, u32[]{:S(2)}) collective-permute-start(bf16[256,1024]{1,0:T(8,128)(2,1)S(1)} %constant_dynamic-update-slice_fusion.2.own_ref), channel_id=1, source_target_pairs={{0,48},{4,20},{8,56},{12,28},{16,0},{20,36},{24,8},{28,44},{32,16}... | collective-permute-start | bytes 1572872 | tf_op jit(solution)/shard_map/ppermute | solution.py:69
  88.0 12.7 %collective-permute-start.30 = (bf16[256,1024]{1,0:T(8,128)(2,1)S(1)}, bf16[256,1024]{1,0:T(8,128)(2,1)S(1)}, u32[]{:S(2)}, u32[]{:S(2)}) collective-permute-start(bf16[256,1024]{1,0:T(8,128)(2,1)S(1)} %constant_dynamic-update-slice_fusion.2.own_ref), channel_id=1, source_target_pairs={{0,16},{4,52},{8,24},{12,60},{16,32},{20,4},{24,40},{28,12},{32,48... | collective-permute-start | bytes 1572872 | tf_op jit(solution)/shard_map/ppermute | solution.py:69
  88.3 1.6 %copy-start.6 = (bf16[4,1024,256]{2,1,0:T(8,128)(2,1)S(1)}, bf16[4,1024,256]{2,1,0:T(8,128)(2,1)}, u32[]{:S(2)}) copy-start(bf16[4,1024,256]{2,1,0:T(8,128)(2,1)} %get-tuple-element.70.o_ref) | copy-start | bytes 6291460
  89.9 0.8 copy-start.7
  100.8 2.8 %collective-permute-start.32 = (bf16[512,1024]{1,0:T(8,128)(2,1)S(1)}, bf16[512,1024]{1,0:T(8,128)(2,1)S(1)}, u32[]{:S(2)}, u32[]{:S(2)}) collective-permute-start(bf16[512,1024]{1,0:T(8,128)(2,1)S(1)} %constant_dynamic-update-slice_fusion.6.own_ref), channel_id=1, source_target_pairs={{0,4},{4,0},{8,12},{12,8},{16,20},{20,16},{24,28},{28,24},{32,36},... | collective-permute-start | bytes 3145736 | tf_op jit(solution)/shard_map/ppermute | solution.py:69
  101.3 11.5 %collective-permute-start.33 = (bf16[256,1024]{1,0:T(8,128)(2,1)S(1)}, bf16[256,1024]{1,0:T(8,128)(2,1)S(1)}, u32[]{:S(2)}, u32[]{:S(2)}) collective-permute-start(bf16[256,1024]{1,0:T(8,128)(2,1)S(1)} %collective-permute-done.30), channel_id=1, source_target_pairs={{0,16},{4,52},{8,24},{12,60},{16,32},{20,4},{24,40},{28,12},{32,48... | collective-permute-start | bytes 1572872 | tf_op jit(solution)/shard_map/ppermute | solution.py:69
  112.8 2.0 %collective-permute-start.34 = (bf16[256,1024]{1,0:T(8,128)(2,1)S(1)}, bf16[256,1024]{1,0:T(8,128)(2,1)S(1)}, u32[]{:S(2)}, u32[]{:S(2)}) collective-permute-start(bf16[256,1024]{1,0:T(8,128)(2,1)S(1)} %collective-permute-done.33.own_ref), channel_id=1, source_target_pairs={{0,4},{4,0},{8,12},{12,8},{16,20},{20,16},{24,28},{28,24},{32,36},... | collective-permute-start | bytes 1572872 | tf_op jit(solution)/shard_map/ppermute | solution.py:69
